TPU v7x, 32 devices: a whole 2x2x4 slice. The times are simulated.
32 devices in a mesh: grp: 2 (over y), mp: 16 (over z, x, core).
Axes of the slice: x: 2, y: 2, z: 4, core: 2. Of those that a mesh axis runs over, the one named last changes fastest.
Arguments:
- query_grad: bfloat16 [64, 8192], P('grp'), parts along dimension 0, may hold values from -0.0625 to 0.0625
- query_input: bfloat16 [64, 8192], P('grp'), parts along dimension 0, may hold values from -6 to 6
- query_ids: int32 [64], P('grp'), parts along dimension 0, may hold values from 0 to 7, never falling along the last dimension, each value on 1 to 8 neighbouring positions
- train_grad: bfloat16 [256, 8192], P('grp'), parts along dimension 0, may hold values from -0.0625 to 0.0625
- train_input: bfloat16 [256, 8192], P('grp'), parts along dimension 0, may hold values from -3 to 3
- train_ids: int32 [256], P('grp'), parts along dimension 0, may hold values from 0 to 15, never falling along the last dimension, each value on 1 to 16 neighbouring positions
- output_basis: bfloat16 [8192, 8192], P(None, 'mp'), may hold values from -0.0625 to 0.0625
- input_basis: bfloat16 [8192, 8192], P(None, 'mp'), may hold values from -0.0625 to 0.0625
- eigenvalues: float32 [8192, 8192], P('mp'), may hold values from 0.05 to 5
Outputs:
- scores: float32 [16, 16], P('grp'), parts along dimension 0
There are 2 independent parts, one for each index of `grp`. A program takes and returns all parts, laid end to end along the dimension named above; an argument that names none is the same for every part. Nothing has to cross between parts.
Inputs may be any that keep to these rules, and one draw needn't show every extreme that they name: `query_ids`: each query is a run of consecutive tokens, 1 to 8 long, one of exactly 8; ids never fall. `train_ids`: each training example is a run of consecutive tokens, 1 to 16 long, one of exactly 16; ids never fall.
All inputs are finite; a program needn't handle non-finite values.
Results may differ from a plain program's by a relative error of at most 0.0049.
Values may be sent and summed in bfloat16 or wider, within the bound.
A program may use at most 256 MiB of HBM per device.

v0:
```python
import math
import jax
import jax.numpy as jnp
from jax import lax
from jax.sharding import PartitionSpec as P

QUERIES = 8
QMOST = 8
TRAIN = 16
damping_shift = 0.25


def rotate(basis, factors):
    return lax.dot_general(
        basis, factors, (((0,), (1,)), ((), ())), preferred_element_type=jnp.float32
    ).astype(jnp.bfloat16)


def query_window(query_ids):
    token_count = query_ids.shape[0]
    labels = jnp.arange(QUERIES, dtype=jnp.int32)
    starts = jnp.sum((query_ids[None, :] < labels[:, None]).astype(jnp.int32), axis=1)
    window = jnp.minimum(
        starts[:, None] + jnp.arange(QMOST, dtype=jnp.int32)[None, :], token_count - 1
    )
    live_slot = jnp.take(query_ids, window) == labels[:, None]
    return (window, live_slot)


def window_rows(columns, window):
    return jnp.transpose(jnp.take(columns, window, axis=1), (1, 2, 0))


def build_precond(left_window, right_cols, eig_cols, window):
    right_window = window_rows(right_cols, window)
    query_count = left_window.shape[0]
    group_size = math.gcd(query_count, 8)
    left_groups = left_window.reshape(
        (query_count // group_size, group_size) + left_window.shape[1:]
    )
    right_groups = right_window.reshape(
        (query_count // group_size, group_size) + right_window.shape[1:]
    )

    def one_group(operands):
        products = jnp.einsum(
            "qms,qma->qsa", operands[0], operands[1], preferred_element_type=jnp.float32
        )
        return (products / (eig_cols[None] + damping_shift)).astype(jnp.bfloat16)

    precond_groups = lax.map(one_group, (left_groups, right_groups))
    return precond_groups.reshape((query_count,) + precond_groups.shape[2:])


def on_device(
    query_grad,
    query_input,
    query_ids,
    train_grad,
    train_input,
    train_ids,
    output_basis,
    input_basis,
    eigenvalues,
):
    query_left = rotate(output_basis, query_grad)
    query_right = rotate(input_basis, query_input)
    train_left = rotate(output_basis, train_grad)
    train_right = rotate(input_basis, train_input)
    window, live_slot = query_window(query_ids)
    left_taken = window_rows(query_left, window)
    left_window = jnp.where(live_slot[:, :, None], left_taken, jnp.zeros((), jnp.bfloat16))
    right_full, train_full = (
        lax.all_gather(query_right, "mp", axis=0, tiled=True),
        lax.all_gather(train_right, "mp", axis=0, tiled=True),
    )
    precond = build_precond(left_window, right_full, eigenvalues, window)
    inner_sum = jnp.einsum("qsa,at->qst", precond, train_full, preferred_element_type=jnp.float32)
    contrib = jnp.einsum(
        "qst,st->qt", inner_sum, train_left.astype(jnp.float32), precision=lax.Precision.HIGHEST
    )
    onehot = (train_ids[:, None] == jnp.arange(TRAIN, dtype=jnp.int32)[None, :]).astype(jnp.float32)
    shares = jnp.dot(contrib, onehot, precision=lax.Precision.HIGHEST)
    return lax.psum(shares, "mp")


def solution(mesh):
    return jax.shard_map(
        on_device,
        mesh=mesh,
        in_specs=(
            P("grp", None),
            P("grp", None),
            P("grp"),
            P("grp", None),
            P("grp", None),
            P("grp"),
            P(None, "mp"),
            P(None, "mp"),
            P("mp", None),
        ),
        out_specs=P("grp", None),
        check_vma=False,
    )
```

profile of v0, /device:TPU:0, one launch (start us, length us, event | category | flops | bytes accessed | tf_op | source)
XLA Modules:
  0.0 167.1 jit_solution(38802841651659386)
XLA Ops:
  6.5 0.0 copy-start
  6.5 0.0 copy-start.1
  6.5 0.0 copy-start.3
  6.5 0.0 all-gather.2.cloned.1.call-start
  6.5 1.6 copy-done
  8.1 6.4 %convolution_convert_fusion = bf16[512,128]{1,0:T(8,128)(2,1)} fusion(bf16[8192,512]{1,0:T(8,128)(2,1)} %param.16, bf16[128,8192]{1,0:T(8,128)(2,1)S(1)} %copy-done), kind=kOutput, calls=%fused_computation.9 | convolution fusion | flops 1073807360 | bytes 10616832 | tf_op jit(solution)/shard_map/dot_general | solution.py:14
  14.5 0.0 all-gather.2.cloned.1.call-update
  14.6 0.0 copy-done.1
  14.6 0.1 convert_reduce_fusion
  14.7 0.1 compare_select_fusion
  14.8 0.1 reshape.101
  14.9 0.8 gather_fusion
  15.6 0.1 reshape.100
  15.7 0.1 iota_compare_fusion.2
  15.8 0.0 copy-done.3
  15.8 4.9 %convolution_convert_fusion.2 = bf16[512,32]{0,1:T(8,128)(2,1)S(1)} fusion(bf16[32,8192]{1,0:T(8,128)(2,1)S(1)} %copy-done.3, bf16[8192,512]{1,0:T(8,128)(2,1)} %param.16), kind=kOutput, calls=%fused_computation.13 | convolution fusion | flops 268451840 | bytes 8945664 | tf_op jit(solution)/shard_map/dot_general | solution.py:14
  20.7 24.6 %all_gather.6 = bf16[8192,32]{0,1:T(8,128)(2,1)S(1)} all-gather(bf16[512,32]{0,1:T(8,128)(2,1)S(1)} %convolution_convert_fusion.2), channel_id=1, replica_groups=mesh['grp'=2,'mp'=16] {'mp'}, dimensions={0}, use_global_device_ids=true | all-gather | bytes 557056 | tf_op jit(solution)/shard_map/all_gather | solution.py:74
  45.4 0.0 copy-start.4
  45.4 2.2 %gather_fusion.2 = bf16[64,8192]{1,0:T(8,128)(2,1)} fusion(bf16[8192,32]{0,1:T(8,128)(2,1)S(1)} %all_gather.6, s32[1024]{0:T(1024)S(1)} %pad_clamp_fusion), kind=kCustom, calls=%fused_computation.2 | custom fusion | bytes 2097408 | tf_op jit(solution)/shard_map/jit(_take)/gather | solution.py:31
  47.6 0.0 copy-done.4
  47.6 4.9 %convolution_convert_fusion.3 = bf16[512,32]{0,1:T(8,128)(2,1)S(1)} fusion(bf16[32,8192]{1,0:T(8,128)(2,1)S(1)} %copy-done.4, bf16[8192,512]{1,0:T(8,128)(2,1)} %param.15), kind=kOutput, calls=%fused_computation.14 | convolution fusion | flops 268451840 | bytes 8945664 | tf_op jit(solution)/shard_map/dot_general | solution.py:14
  52.5 0.7 gather_fusion.1
  53.2 0.0 copy-start.2
  53.2 11.9 %broadcast_add_fusion = f32[512,8192]{1,0:T(8,128)} fusion(f32[512,8192]{1,0:T(8,128)} %param.17), kind=kLoop, calls=%fused_computation.6 | loop fusion | flops 4194304 | bytes 33554432 | tf_op jit(solution)/shard_map/while/body/eval_jaxpr/add | solution.py:49
  65.1 0.0 copy-done.2
  65.1 30.2 %divide_convert_fusion.6 = bf16[8,512,8192]{2,1,0:T(8,128)(2,1)} fusion(f32[512,8192]{1,0:T(8,128)} %broadcast_add_fusion, bf16[64,8192]{1,0:T(8,128)(2,1)S(1)} %copy-done.2, pred[8,8]{1,0:T(8,128)(4,1)S(1)} %get-tuple-element.14, bf16[64,512]{1,0:T(8,128)(2,1)S(1)} %gather_fusion.1, pred[8,8]{1,0:T(8,128)(4,1)S(1)} %get-tuple-element.13), kind=kOutput, calls=%fused_computation.3.clone.clone.clone.clone.1 | convolution fusion | flops 604569600 | bytes 85000320 | tf_op jit(solution)/shard_map/while/body/eval_jaxpr/qms,qma->qsa/dot_general | solution.py:46
  95.3 6.3 %fusion.7 = f32[128,512]{0,1:T(8,128)S(1)} fusion(bf16[8192,512]{1,0:T(8,128)(2,1)} %param.15, bf16[128,8192]{1,0:T(8,128)(2,1)} %param.12), kind=kOutput, calls=%fused_computation.12 | convolution fusion | flops 1073872896 | bytes 10747904 | tf_op jit(solution)/shard_map/dot_general | solution.py:14
  101.7 0.0 copy-start.5
  101.7 0.0 all-gather.2.cloned.1.call-done
  101.7 27.9 %multiply_reduce_fusion = f32[128,8]{0,1:T(8,128)S(1)} fusion(bf16[8192,128]{1,0:T(8,128)(2,1)} %all-gather.2.cloned.1.call-done, f32[128,512]{0,1:T(8,128)S(1)} %fusion.7, bf16[8,512,8192]{2,1,0:T(8,128)(2,1)} %divide_convert_fusion.6), kind=kOutput, calls=%fused_computation.8 | convolution fusion | flops 8590982144 | bytes 69472256 | tf_op jit(solution)/shard_map/qsa,at->qst/dot_general | solution.py:78
  129.6 0.0 copy-done.5
  129.7 0.2 fusion.19
  129.8 30.4 %psum.7 = f32[8,16]{1,0:T(8,128)} all-reduce(f32[8,16]{1,0:T(8,128)S(1)} %fusion.19), channel_id=1, replica_groups=mesh['grp'=2,'mp'=16] {'mp'}, use_global_device_ids=true, to_apply=%region_1.2 | all-reduce | flops 128 | bytes 1024 | tf_op jit(solution)/shard_map/psum | solution.py:84
  (1 shorter events, 0.0 us)
Async XLA Ops:
  6.5 1.6 copy-start
  6.5 8.0 %copy-start.1 = (s32[32]{0:T(128)S(1)}, s32[32]{0:T(128)}, u32[]{:S(2)}) copy-start(s32[32]{0:T(128)} %param.11) | copy-start | bytes 388
  6.5 9.3 %copy-start.3 = (bf16[32,8192]{1,0:T(8,128)(2,1)S(1)}, bf16[32,8192]{1,0:T(8,128)(2,1)}, u32[]{:S(2)}) copy-start(bf16[32,8192]{1,0:T(8,128)(2,1)} %param.10) | copy-start | bytes 1572868
  6.5 95.2 %all-gather.2.cloned.1.call-start = ((), (), s32[]{:S(2)}) async-start(), calls=%async_computation | async-start | bytes 2228224 | tf_op jit(solution)/shard_map/all_gather | solution.py:75
  45.4 2.2 %copy-start.4 = (bf16[32,8192]{1,0:T(8,128)(2,1)S(1)}, bf16[32,8192]{1,0:T(8,128)(2,1)}, u32[]{:S(2)}) copy-start(bf16[32,8192]{1,0:T(8,128)(2,1)} %param.9) | copy-start | bytes 1572868
  53.2 11.9 %copy-start.2 = (bf16[64,8192]{1,0:T(8,128)(2,1)S(1)}, bf16[64,8192]{1,0:T(8,128)(2,1)}, u32[]{:S(2)}) copy-start(bf16[64,8192]{1,0:T(8,128)(2,1)} %gather_fusion.2) | copy-start | bytes 3145732
  101.7 28.0 %copy-start.5 = (s32[128]{0:T(128)S(1)}, s32[128]{0:T(128)}, u32[]{:S(2)}) copy-start(s32[128]{0:T(128)} %param.14) | copy-start | bytes 1540
Sparse Core Ops, SparseCore 0:
  14.7 44.4 all-gather.1
where the time goes:
time: 167 us
  matrix products  81 us (49%)
  blocking collectives  55.1 us (33%)
  between operations  13.5 us (8%)
  other arithmetic  12.1 us (7%)
  local copies, waits for them, and re-layouts  5.45 us (3%)
    psum x1, blocking collectives, on_device(): return lax.psum(shares, 'mp')  30.4 us
    dot_general x1, matrix products, one_group(): jnp.einsum('qms,qma->qsa', operands[0], operands[1], preferred_element_ty...  30.2 us
    dot_general x1, matrix products, on_device(): jnp.einsum('qsa,at->qst', precond, train_full, preferred_element_type=jnp...  27.9 us
    all_gather x1, blocking collectives, on_device(): lax.all_gather(query_right, 'mp', axis=0, tiled=True)  24.6 us
    dot_general x4, matrix products, rotate(): lax.dot_general(basis, factors, (((0,), (1,)), ((), ())), preferred_eleme...  22.6 us
    add x1, other arithmetic, one_group(): return (products / (eig_cols[None] + damping_shift)).astype(jnp.bfloat16)  11.9 us
  transfers between devices with their start and end apart: 1, of which 0 were waited for; matrix products, arithmetic and copies ran while one was open for 37% of the time, Pallas kernels for 0%

commit v1 on v0

--- a/solution.py
+++ b/solution.py
@@ -8,6 +8,18 @@
 QMOST = 8
 TRAIN = 16
 damping_shift = 0.25
+
+
+def doubled_up(array, axis, dim):
+    ways, here, hop = (lax.axis_size(axis), lax.axis_index(axis), array.shape[dim])
+    line, have = (array, 1)
+    while have < ways:
+        line = jnp.concatenate(
+            [line, lax.ppermute(line, axis, [(d, (d - have) % ways) for d in range(ways)])],
+            axis=dim,
+        )
+        have = 2 * have
+    return jnp.roll(line, here * hop, axis=dim)
 
 
 def rotate(basis, factors):
@@ -71,7 +83,7 @@
     left_taken = window_rows(query_left, window)
     left_window = jnp.where(live_slot[:, :, None], left_taken, jnp.zeros((), jnp.bfloat16))
     right_full, train_full = (
-        lax.all_gather(query_right, "mp", axis=0, tiled=True),
+        doubled_up(query_right, "mp", 0),
         lax.all_gather(train_right, "mp", axis=0, tiled=True),
     )
     precond = build_precond(left_window, right_full, eigenvalues, window)

time: 167 us -> 178 us (1.066)
  blocking collectives: 55.1 us -> 33.8 us
  waiting for transfers between devices: 0.04 us -> 20.9 us
  starting transfers between devices: 0.01 us -> 7.07 us
  local copies, waits for them, and re-layouts: 5.45 us -> 10.8 us
    all_gather x1 -> x0, blocking collectives: 24.6 us -> none  [on_device(): lax.all_gather(query_right, 'mp', axis=0, tiled=True)]
    ppermute x0 -> x4, waiting for transfers between devices: none -> 20.9 us  [doubled_up(): lax.ppermute(line, axis, [(d, (d - have) % ways) for d in range(ways)])]
    ppermute x0 -> x4, starting transfers between devices: none -> 7.07 us  [doubled_up(): lax.ppermute(line, axis, [(d, (d - have) % ways) for d in range(ways)])]
    unnamed x12 -> x22, local copies, waits for them, and re-layouts: 1.61 us -> 5.19 us
    psum x1, blocking collectives: 30.4 us -> 33.8 us  [on_device(): return lax.psum(shares, 'mp')]
    dot_general x4, matrix products: 22.6 us -> 20.3 us  [rotate(): lax.dot_general(basis, factors, (((0,), (1,)), ((), ())), preferred_eleme...]
  transfers between devices with their start and end apart: 1 -> 5, of which waited for: 0 -> 3; matrix products, arithmetic and copies ran while one was open for 37% -> 39% of each run, Pallas kernels for 0% -> 0%
where the time goes in v1:
time: 178 us
  matrix products  79.6 us (45%)
  blocking collectives  33.8 us (19%)
  waiting for transfers between devices  20.9 us (12%)
  between operations  13.5 us (8%)
  other arithmetic  12 us (7%)
  local copies, waits for them, and re-layouts  10.8 us (6%)
  starting transfers between devices  7.07 us (4%)
    psum x1, blocking collectives, on_device(): return lax.psum(shares, 'mp')  33.8 us
    dot_general x1, matrix products, one_group(): jnp.einsum('qms,qma->qsa', operands[0], operands[1], preferred_element_ty...  31.1 us
    dot_general x1, matrix products, on_device(): jnp.einsum('qsa,at->qst', precond, train_full, preferred_element_type=jnp...  27.9 us
    ppermute x4, waiting for transfers between devices, doubled_up(): lax.ppermute(line, axis, [(d, (d - have) % ways) for d in range(ways)])  20.9 us
    dot_general x4, matrix products, rotate(): lax.dot_general(basis, factors, (((0,), (1,)), ((), ())), preferred_eleme...  20.3 us
    add x1, other arithmetic, one_group(): return (products / (eig_cols[None] + damping_shift)).astype(jnp.bfloat16)  11.6 us
    ppermute x4, starting transfers between devices, doubled_up(): lax.ppermute(line, axis, [(d, (d - have) % ways) for d in range(ways)])  7.07 us
    unnamed x22, local copies, waits for them, and re-layouts  5.19 us
  transfers between devices with their start and end apart: 5, of which 3 were waited for; matrix products, arithmetic and copies ran while one was open for 39% of the time, Pallas kernels for 0%

profile of v1, /device:TPU:0, one launch (start us, length us, event | category | flops | bytes accessed | tf_op | source)
XLA Modules:
  0.0 177.6 jit_solution(11696945178573772565)
XLA Ops:
  6.5 0.0 copy-start
  6.5 0.0 all-gather.2.cloned.1.call-start
  6.5 0.0 copy-start.2
  6.5 5.8 %constant_dynamic-update-slice_fusion.9 = (bf16[16384,32]{0,1:T(8,128)(2,1)}, bf16[512,32]{0,1:T(8,128)(2,1)S(1)}) fusion(bf16[32,8192]{1,0:T(8,128)(2,1)} %param.10, bf16[8192,512]{1,0:T(8,128)(2,1)} %param.16), kind=kOutput, calls=%fused_computation.39 | convolution fusion | flops 268451840 | bytes 8978432 | tf_op jit(solution)/shard_map/dot_general | solution.py:26
  12.4 0.0 copy-start.1
  12.4 5.4 %collective-permute-start = (bf16[512,32]{0,1:T(8,128)(2,1)S(1)}, bf16[512,32]{0,1:T(8,128)(2,1)S(1)}, u32[]{:S(2)}, u32[]{:S(2)}) collective-permute-start(bf16[512,32]{0,1:T(8,128)(2,1)S(1)} %get-tuple-element.22), channel_id=1, source_target_pairs={{0,15},{1,0},{2,1},{3,2},{4,3},{5,4},{6,5},{7,6},{8,7},{9,8},{10,9... | collective-permute-start | bytes 98312 | tf_op jit(solution)/shard_map/ppermute | solution.py:18
  17.8 0.0 copy-done
  17.8 0.0 copy-done.2
  17.8 3.0 %convolution_convert_fusion = bf16[512,128]{1,0:T(8,128)(2,1)} fusion(bf16[8192,512]{1,0:T(8,128)(2,1)S(1)} %copy-done.2, bf16[128,8192]{1,0:T(8,128)(2,1)S(1)} %copy-done), kind=kOutput, calls=%fused_computation.9 | convolution fusion | flops 1073807360 | bytes 10616832 | tf_op jit(solution)/shard_map/dot_general | solution.py:26
  20.8 0.0 all-gather.2.cloned.1.call-update
  20.8 0.0 copy-done.1
  20.9 0.1 convert_reduce_fusion
  21.0 0.0 copy-start.3
  21.0 11.6 %broadcast_add_fusion = f32[512,8192]{1,0:T(8,128)} fusion(f32[512,8192]{1,0:T(8,128)} %param.17), kind=kLoop, calls=%fused_computation.6 | loop fusion | flops 4194304 | bytes 33554432 | tf_op jit(solution)/shard_map/while/body/eval_jaxpr/add | solution.py:61
  32.6 0.0 copy-done.3
  32.6 5.0 %convolution_convert_fusion.3 = bf16[512,32]{0,1:T(8,128)(2,1)S(1)} fusion(bf16[32,8192]{1,0:T(8,128)(2,1)S(1)} %copy-done.3, bf16[8192,512]{1,0:T(8,128)(2,1)} %param.15), kind=kOutput, calls=%fused_computation.14 | convolution fusion | flops 268451840 | bytes 8945664 | tf_op jit(solution)/shard_map/dot_general | solution.py:26
  37.7 0.0 copy-done.4
  37.7 6.4 %fusion.7 = f32[128,512]{0,1:T(8,128)} fusion(bf16[8192,512]{1,0:T(8,128)(2,1)} %param.15, bf16[128,8192]{1,0:T(8,128)(2,1)S(1)} %copy-done.4), kind=kOutput, calls=%fused_computation.12 | convolution fusion | flops 1073872896 | bytes 10747904 | tf_op jit(solution)/shard_map/dot_general | solution.py:26
  44.1 0.1 compare_select_fusion
  44.2 0.1 reshape.101
  44.3 0.0 collective-permute-done
  44.3 1.3 collective-permute-start.1
  45.6 0.8 gather_fusion
  46.4 0.1 reshape.100
  46.5 3.5 %collective-permute-done.1 = bf16[1024,32]{0,1:T(8,128)(2,1)S(1)} collective-permute-done((bf16[1024,32]{0,1:T(8,128)(2,1)S(1)}, bf16[1024,32]{0,1:T(8,128)(2,1)S(1)}, u32[]{:S(2)}, u32[]{:S(2)}) %collective-permute-start.1) | collective-permute-done | bytes 65568 | tf_op jit(solution)/shard_map/ppermute | solution.py:18
  50.0 0.2 collective-permute-start.2
  50.2 0.1 iota_compare_fusion.2
  50.3 0.7 gather_fusion.1
  51.0 0.6 constant_dynamic-update-slice_fusion.8
  51.6 5.6 %collective-permute-done.2 = bf16[2048,32]{0,1:T(8,128)(2,1)S(1)} collective-permute-done((bf16[2048,32]{0,1:T(8,128)(2,1)S(1)}, bf16[2048,32]{0,1:T(8,128)(2,1)S(1)}, u32[]{:S(2)}, u32[]{:S(2)}) %collective-permute-start.2) | collective-permute-done | bytes 131104 | tf_op jit(solution)/shard_map/ppermute | solution.py:18
  57.3 0.1 collective-permute-start.3
  57.3 0.6 constant_dynamic-update-slice_fusion.7
  58.0 0.7 constant_dynamic-update-slice_fusion.6
  58.6 11.8 %collective-permute-done.3 = bf16[4096,32]{0,1:T(8,128)(2,1)S(1)} collective-permute-done((bf16[4096,32]{0,1:T(8,128)(2,1)S(1)}, bf16[4096,32]{0,1:T(8,128)(2,1)S(1)}, u32[]{:S(2)}, u32[]{:S(2)}) %collective-permute-start.3) | collective-permute-done | bytes 262176 | tf_op jit(solution)/shard_map/ppermute | solution.py:18
  70.4 0.7 constant_dynamic-update-slice_fusion.5
  71.2 0.6 constant_dynamic-update-slice_fusion.4
  71.8 0.6 constant_dynamic-update-slice_fusion.3
  72.4 0.6 constant_dynamic-update-slice_fusion.2
  73.0 0.7 constant_dynamic-update-slice_fusion.1
  73.7 0.7 constant_dynamic-update-slice_fusion
  74.4 1.1 constant_dynamic-slice_fusion
  75.5 2.2 %gather_fusion.2 = bf16[64,8192]{1,0:T(8,128)(2,1)} fusion(bf16[8192,32]{0,1:T(8,128)(2,1)S(1)} %constant_dynamic-slice_fusion, s32[1024]{0:T(1024)S(1)} %pad_clamp_fusion), kind=kCustom, calls=%fused_computation.2 | custom fusion | bytes 2097408 | tf_op jit(solution)/shard_map/jit(_take)/gather | solution.py:43
  77.7 31.1 %divide_convert_fusion.6 = bf16[8,512,8192]{2,1,0:T(8,128)(2,1)} fusion(f32[512,8192]{1,0:T(8,128)} %broadcast_add_fusion, bf16[64,8192]{1,0:T(8,128)(2,1)} %gather_fusion.2, pred[8,8]{1,0:T(8,128)(4,1)S(1)} %get-tuple-element.14, bf16[64,512]{1,0:T(8,128)(2,1)S(1)} %gather_fusion.1, pred[8,8]{1,0:T(8,128)(4,1)S(1)} %get-tuple-element.13), kind=kOutput, calls=%fused_computation.3.clone.clone.clone.clone.1 | convolution fusion | flops 604569600 | bytes 85000320 | tf_op jit(solution)/shard_map/while/body/eval_jaxpr/qms,qma->qsa/dot_general | solution.py:58
  108.9 0.0 copy-done.6
  108.9 27.9 %multiply_reduce_fusion = f32[128,8]{0,1:T(8,128)S(1)} fusion(bf16[8192,128]{1,0:T(8,128)(2,1)} %all-gather.2.cloned.1.call-done, f32[128,512]{0,1:T(8,128)S(1)} %copy-done.6, bf16[8,512,8192]{2,1,0:T(8,128)(2,1)} %divide_convert_fusion.6), kind=kOutput, calls=%fused_computation.8 | convolution fusion | flops 8590982144 | bytes 69472256 | tf_op jit(solution)/shard_map/qsa,at->qst/dot_general | solution.py:90
  136.8 0.0 copy-done.5
  136.8 0.2 fusion.19
  137.0 33.8 %psum.7 = f32[8,16]{1,0:T(8,128)} all-reduce(f32[8,16]{1,0:T(8,128)S(1)} %fusion.19), channel_id=1, replica_groups=mesh['grp'=2,'mp'=16] {'mp'}, use_global_device_ids=true, to_apply=%region_1.2 | all-reduce | flops 128 | bytes 1024 | tf_op jit(solution)/shard_map/psum | solution.py:96
  (8 shorter events, 0.0 us)
Async XLA Ops:
  6.5 11.3 %copy-start = (bf16[128,8192]{1,0:T(8,128)(2,1)S(1)}, bf16[128,8192]{1,0:T(8,128)(2,1)}, u32[]{:S(2)}) copy-start(bf16[128,8192]{1,0:T(8,128)(2,1)} %param.13) | copy-start | bytes 6291460
  6.5 102.3 %all-gather.2.cloned.1.call-start = ((), (), s32[]{:S(2)}) async-start(), calls=%async_computation | async-start | bytes 2228224 | tf_op jit(solution)/shard_map/all_gather | solution.py:87
  6.5 11.3 %copy-start.2 = (bf16[8192,512]{1,0:T(8,128)(2,1)S(1)}, bf16[8192,512]{1,0:T(8,128)(2,1)}, u32[]{:S(2)}) copy-start(bf16[8192,512]{1,0:T(8,128)(2,1)} %param.16) | copy-start | bytes 25165828
  12.4 8.5 %copy-start.1 = (s32[32]{0:T(128)S(1)}, s32[32]{0:T(128)}, u32[]{:S(2)}) copy-start(s32[32]{0:T(128)} %param.11) | copy-start | bytes 388
  12.4 31.9 %collective-permute-start = (bf16[512,32]{0,1:T(8,128)(2,1)S(1)}, bf16[512,32]{0,1:T(8,128)(2,1)S(1)}, u32[]{:S(2)}, u32[]{:S(2)}) collective-permute-start(bf16[512,32]{0,1:T(8,128)(2,1)S(1)} %get-tuple-element.22), channel_id=1, source_target_pairs={{0,15},{1,0},{2,1},{3,2},{4,3},{5,4},{6,5},{7,6},{8,7},{9,8},{10,9... | collective-permute-start | bytes 98312 | tf_op jit(solution)/shard_map/ppermute | solution.py:18
  21.0 11.7 %copy-start.3 = (bf16[32,8192]{1,0:T(8,128)(2,1)S(1)}, bf16[32,8192]{1,0:T(8,128)(2,1)}, u32[]{:S(2)}) copy-start(bf16[32,8192]{1,0:T(8,128)(2,1)} %param.9) | copy-start | bytes 1572868
  32.6 5.1 %copy-start.4 = (bf16[128,8192]{1,0:T(8,128)(2,1)S(1)}, bf16[128,8192]{1,0:T(8,128)(2,1)}, u32[]{:S(2)}) copy-start(bf16[128,8192]{1,0:T(8,128)(2,1)} %param.12) | copy-start | bytes 6291460
  44.3 5.7 %collective-permute-start.1 = (bf16[1024,32]{0,1:T(8,128)(2,1)S(1)}, bf16[1024,32]{0,1:T(8,128)(2,1)S(1)}, u32[]{:S(2)}, u32[]{:S(2)}) collective-permute-start(bf16[1024,32]{0,1:T(8,128)(2,1)S(1)} %pad_maximum_fusion.2), channel_id=1, source_target_pairs={{0,14},{1,15},{2,0},{3,1},{4,2},{5,3},{6,4},{7,5},{8,6},{9,7},{10,... | collective-permute-start | bytes 196616 | tf_op jit(solution)/shard_map/ppermute | solution.py:18
  50.0 7.3 %collective-permute-start.2 = (bf16[2048,32]{0,1:T(8,128)(2,1)S(1)}, bf16[2048,32]{0,1:T(8,128)(2,1)S(1)}, u32[]{:S(2)}, u32[]{:S(2)}) collective-permute-start(bf16[2048,32]{0,1:T(8,128)(2,1)S(1)} %pad_maximum_fusion.1), channel_id=1, source_target_pairs={{0,12},{1,13},{2,14},{3,15},{4,0},{5,1},{6,2},{7,3},{8,4},{9,5},{1... | collective-permute-start | bytes 393224 | tf_op jit(solution)/shard_map/ppermute | solution.py:18
  57.3 13.2 %collective-permute-start.3 = (bf16[4096,32]{0,1:T(8,128)(2,1)S(1)}, bf16[4096,32]{0,1:T(8,128)(2,1)S(1)}, u32[]{:S(2)}, u32[]{:S(2)}) collective-permute-start(bf16[4096,32]{0,1:T(8,128)(2,1)S(1)} %pad_maximum_fusion), channel_id=1, source_target_pairs={{0,8},{1,9},{2,10},{3,11},{4,12},{5,13},{6,14},{7,15},{8,0},{9,1},... | collective-permute-start | bytes 786440 | tf_op jit(solution)/shard_map/ppermute | solution.py:18
  77.7 31.2 %copy-start.6 = (f32[128,512]{0,1:T(8,128)S(1)}, f32[128,512]{0,1:T(8,128)}, u32[]{:S(2)}) copy-start(f32[128,512]{0,1:T(8,128)} %fusion.7) | copy-start | bytes 786436
  108.9 27.9 %copy-start.5 = (s32[128]{0:T(128)S(1)}, s32[128]{0:T(128)}, u32[]{:S(2)}) copy-start(s32[128]{0:T(128)} %param.14) | copy-start | bytes 1540
Sparse Core Ops, SparseCore 0:
  21.0 41.8 all-gather.1
